TPU v7x, 128 devices: a whole 4x4x4 slice. The times are simulated.
128 devices in a mesh: ctx: 64 (over x, y, z_hi, core), tp: 2 (over z_lo).
Axes of the slice: x: 4, y: 4, z: 4 (z_hi: 2, z_lo: 2; z = z_hi * 2 + z_lo), core: 2. Of those that a mesh axis runs over, the one named last changes fastest.
Arguments:
- queries: bfloat16 [16384, 4096], P(('ctx', 'tp')), may hold values from -5 to 5
- keys: bfloat16 [16384, 512], P(('ctx', 'tp')), may hold values from -5 to 5
- values: bfloat16 [16384, 512], P(('ctx', 'tp')), may hold values from -6 to 6
- d_out: bfloat16 [16384, 4096], P(('ctx', 'tp')), may hold values from -6 to 6
- lengths: int32 [64], replicated, may hold values from 64 to 256, as said below
- ancestors: int32 [64, 7], P('ctx'), may hold values from 0 to 1, as said below
- rewards: float32 [64], P('ctx'), may hold values from -11 to 11
- pruned: int32 [64], P('ctx'), may hold values 0 or 1
- branch_group: int32 [64], P('ctx'), may hold values from 0 to 7
Outputs:
- attended: bfloat16 [16384, 4096], P(('ctx', 'tp'))
- grad_queries: bfloat16 [16384, 4096], P(('ctx', 'tp'))
- grad_keys: bfloat16 [16384, 512], P(('ctx', 'tp'))
- grad_values: bfloat16 [16384, 512], P(('ctx', 'tp'))
- advantage: float32 [64], P('ctx')
Inputs may be any that keep to these rules, and one draw needn't show every extreme that they name: Segments form trees of 8 consecutive segments starting at multiples of 8; ancestors[s, o - 1] is 1 when segment s - o is an ancestor of segment s in its tree. The first segment of a tree is an ancestor of all others; every segment has at most two ancestors. `lengths`: the first segment of every tree is full.
All inputs are finite; a program needn't handle non-finite values. No bound on the sum of `pruned` on one device may be relied on, other than what follows from the above.
Results may differ from a plain program's by a relative error of at most 0.02.
Values may be sent and summed in bfloat16 or wider, within the bound.
A program may use at most 192 MiB of HBM per device.

v0:
```python
import jax
import jax.numpy as jnp
from jax import lax
from jax.experimental import pallas as pl
from jax.experimental.pallas import tpu as pltpu
from jax.sharding import PartitionSpec as P

H = 32
KVH = 4
HD = 128
TILE = 256
HALF = 128
TREE = 8
GROUPS = 8
WIDE = 256
MESH = pl.DeviceIdType.MESH
SCALE = HD**-0.5
LOG2 = SCALE * 1.4426950408889634
NEG = -1e30
f32 = jnp.float32
bf16 = jnp.bfloat16
NT = (((1,), (1,)), ((), ()))
PARTS = ((0, 48), (48, 48), (96, 32))


def cols(index, size):
    return pl.ds(pl.multiple_of(index * size, size), size)


def dot(a, b):
    return jnp.dot(a, b, preferred_element_type=f32)


def dot_nt(a, b):
    return lax.dot_general(a, b, NT, preferred_element_type=f32)


def kernel(
    q_hbm, k_hbm, v_hbm, do_hbm, len_ref, anc_ref, rew_ref, pru_ref, grp_ref,
    att_hbm, dq_hbm, gk_ref, gv_ref, adv_ref,
    q_ref, do_ref, att_ref, dq_ref, kv, qT, doT, e_ref, oT, dqT, st, bias,
    near, far, total, mine, theirs, inbox, outbox,
    loc_sem, ag_send, ag_recv, core_send, core_recv, st_send, st_recv, rs_send, rs_recv,
):
    ctx = lax.axis_index("ctx")
    tp = lax.axis_index("tp")
    tree = ctx // TREE
    seg = ctx % TREE
    core = ctx % 2
    z = ((ctx // 2) % 2) * 2 + tp
    y = (ctx // 4) % 2
    first = tree * TREE

    def place(yy, zz, cc):
        zz = zz % 4
        return first + yy * 4 + (zz // 2) * 2 + cc, zz % 2

    def segment(yy, zz):
        zz = zz % 4
        return yy * 4 + (zz // 2) * 2 + core

    dev_core = place(y, z, 1 - core)
    dev_up = place(y, z + 1, core)
    dev_down = place(y, z + 3, core)
    dev_y = place(1 - y, z, core)
    links = (dev_up, dev_down, dev_y)
    kin = [(first + (seg + i) % TREE, tp) for i in range(1, TREE)]
    others = [(((tree + i) % 8) * TREE + seg, tp) for i in range(1, 8)]

    barrier = pltpu.get_barrier_semaphore()
    for device in kin + [dev_up, dev_down] + others:
        pl.semaphore_signal(barrier, inc=1, device_id=device, device_id_type=MESH)

    own_rows = pl.ds(tp * HALF, HALF)
    loads = [
        pltpu.make_async_copy(k_hbm, kv.at[seg, 0, own_rows], loc_sem.at[0]),
        pltpu.make_async_copy(v_hbm, kv.at[seg, 1, own_rows], loc_sem.at[1]),
        pltpu.make_async_copy(q_hbm, q_ref, loc_sem.at[2]),
        pltpu.make_async_copy(do_hbm, do_ref, loc_sem.at[3]),
    ]
    for load in loads:
        load.start()

    lane = lax.broadcasted_iota(jnp.int32, (8, 128), 1)
    row = lax.broadcasted_iota(jnp.int32, (8, 128), 0)
    reward = rew_ref[0]
    living = 1.0 - pru_ref[0].astype(f32)
    belongs = lane == grp_ref[0]
    parent = jnp.int32(0)
    for o in range(1, TREE):
        parent = parent + jnp.where(o < seg, anc_ref[0, o - 1] * (seg - o), 0)
    has_parent = parent > 0
    terms = jnp.where(row == 0, living, jnp.where(row == 1, living * reward, living * reward * reward))
    near[0] = jnp.where(
        row < 3, jnp.where(belongs, terms, 0.0), jnp.where(has_parent, parent, -1).astype(f32)
    )

    pl.semaphore_wait(barrier, 16)
    loads[0].wait()
    loads[1].wait()

    def block(yy, zz, start=0, size=HALF):
        zz = zz % 4
        return kv.at[segment(yy, zz), :, pl.ds(pl.multiple_of((zz % 2) * HALF + start, 16), size)]

    def send(ref, i, device, sends=ag_send, recvs=ag_recv):
        copy = pltpu.make_async_remote_copy(
            src_ref=ref, dst_ref=ref, send_sem=sends.at[i], recv_sem=recvs.at[i],
            device_id=device, device_id_type=MESH,
        )
        copy.start()
        return copy

    def forward(ref, i):
        return send(ref, i, dev_core, core_send, core_recv)

    ag = [send(block(y, z), i, links[i]) for i in range(3)]
    cores = [forward(block(y, z), 0)]
    notes = []
    for i in range(1, TREE):
        copy = pltpu.make_async_remote_copy(
            src_ref=near.at[0], dst_ref=near.at[i], send_sem=st_send.at[i], recv_sem=st_recv.at[i],
            device_id=kin[i - 1], device_id_type=MESH,
        )
        copy.start()
        notes.append(copy)

    own_len = len_ref[ctx]
    par_len = jnp.where(has_parent, len_ref[first + parent], 0)
    u = lax.broadcasted_iota(jnp.int32, (TILE, HALF), 0)
    t = lax.broadcasted_iota(jnp.int32, (TILE, HALF), 1) + tp * HALF
    bias[0] = jnp.where((u <= t) & (u < own_len), 0.0, NEG)
    bias[1] = jnp.where(u < par_len, 0.0, NEG)
    root_off = jnp.where(seg > 0, 0.0, -NEG)
    loads[2].wait()
    loads[3].wait()

    def turn(h, carry):
        qT[:, cols(h, HD)] = q_ref[:, cols(h, HD)].T
        doT[:, cols(h, HD)] = do_ref[:, cols(h, HD)].T
        return carry

    lax.fori_loop(0, H, turn, 0, unroll=4)

    for copy in notes:
        copy.wait_recv()
    summed = near[0]
    for i in range(1, TREE):
        summed = summed + near[i]
    far[0] = summed
    mate = jnp.where(core == 0, near[7], near[1])[3:4, 0:1]
    more = []
    for i in range(1, 8):
        copy = pltpu.make_async_remote_copy(
            src_ref=far.at[0], dst_ref=far.at[i], send_sem=st_send.at[7 + i],
            recv_sem=st_recv.at[7 + i], device_id=others[i - 1], device_id_type=MESH,
        )
        copy.start()
        more.append(copy)

    for copy in ag:
        copy.wait_recv()
    second = [
        send(block(1 - y, z), 3, dev_up),
        send(block(y, z + 1), 4, dev_down),
        send(block(y, z + 1), 5, dev_y),
    ]
    cores += [
        forward(block(y, z + 3), 1),
        forward(block(y, z + 1), 2),
        forward(block(1 - y, z), 3),
    ]

    def forward_own(k, carry):
        ko = kv[seg, 0, :, cols(k, HD)]
        vT = kv[seg, 1, :, cols(k, HD)].T
        b = jnp.concatenate([bias[0], bias[0]], 1)
        for p in range(4):
            c = cols(k * 4 + p, WIDE)
            s = dot(ko, qT[:, c]) + b
            m = jnp.max(s, 0, keepdims=True) * LOG2
            e = jnp.exp2(s * LOG2 - m)
            st[0:1, c] = m
            st[1:2, c] = jnp.sum(e, 0, keepdims=True)
            e = e.astype(bf16)
            e_ref[0:TILE, c] = e
            oT[:, c] = dot(vT, e)
        return carry

    lax.fori_loop(0, KVH, forward_own, 0)

    for copy in second:
        copy.wait_recv()
    (a0, an), (b0, bn), (c0, cn) = PARTS
    third = [
        send(block(1 - y, z + 3, b0, bn), 6, dev_up),
        send(block(1 - y, z + 1, a0, an), 7, dev_down),
        send(block(y, z + 2, c0, cn), 8, dev_y),
    ]
    cores += [
        forward(block(1 - y, z + 3), 4),
        forward(block(y, z + 2), 5),
        forward(block(1 - y, z + 1), 6),
    ]
    for copy in more:
        copy.wait_recv()
    summed = far[0]
    for i in range(1, 8):
        summed = summed + far[i]
    members = jnp.maximum(summed[0:1], 1.0)
    average = summed[1:2] / members
    spread = jnp.sqrt(jnp.maximum(summed[2:3] / members - average * average, 0.0))
    here = belongs[0:1]
    adv = (
        living
        * (reward - jnp.sum(jnp.where(here, average, 0.0), 1, keepdims=True))
        / jnp.sum(jnp.where(here, jnp.maximum(spread, 1.0), 0.0), 1, keepdims=True)
    )
    adv_ref[...] = jnp.broadcast_to(adv, (1, 128))
    for copy in third:
        copy.wait_recv()
    cores += [
        forward(block(1 - y, z + 2, b0, bn), 7),
        forward(block(1 - y, z + 2, a0, an), 8),
        forward(block(1 - y, z + 2, c0, cn), 9),
    ]
    for copy in cores:
        copy.wait_recv()
    for copy in ag + second + third + cores + notes + more:
        copy.wait_send()

    def forward_rest(k, carry):
        kr = kv[0, 0, :, cols(k, HD)]
        kp = kv[parent, 0, :, cols(k, HD)]
        vT = jnp.concatenate([kv[0, 1, :, cols(k, HD)], kv[parent, 1, :, cols(k, HD)]], 0).T
        b = jnp.concatenate([bias[1], bias[1]], 1)
        slot = lax.broadcasted_iota(jnp.int32, (1, WIDE), 1) % HALF + tp * HALF
        for p in range(4):
            c = cols(k * 4 + p, WIDE)
            sr = dot(kr, qT[:, c])
            sp = dot(kp, qT[:, c]) + b
            m2 = (
                jnp.maximum(jnp.max(sr, 0, keepdims=True) - root_off, jnp.max(sp, 0, keepdims=True))
                * LOG2
            )
            er = jnp.exp2(sr * LOG2 - (m2 + root_off))
            ep = jnp.exp2(sp * LOG2 - m2)
            l2 = jnp.sum(er, 0, keepdims=True) + jnp.sum(ep, 0, keepdims=True)
            e = jnp.concatenate([er, ep], 0).astype(bf16)
            e_ref[TILE : 3 * TILE, c] = e
            o2 = dot(vT, e)
            m1 = st[0:1, c]
            m = jnp.maximum(m1, m2)
            a1 = jnp.exp2(m1 - m)
            a2 = jnp.exp2(m2 - m)
            inv = jnp.where(slot < own_len, 1.0 / (st[1:2, c] * a1 + l2 * a2), 0.0)
            s1 = a1 * inv
            s2 = a2 * inv
            o = oT[:, c] * s1 + o2 * s2
            st[2:3, c] = s1
            st[3:4, c] = s2
            st[4:5, c] = jnp.sum(o * doT[:, c].astype(f32), 0, keepdims=True)
            o = o.T
            for i in range(2):
                att_ref[:, cols((k * 4 + p) * 2 + i, HD)] = o[i * HD : (i + 1) * HD].astype(bf16)
        return carry

    lax.fori_loop(0, KVH, forward_rest, 0)
    store_att = pltpu.make_async_copy(att_ref, att_hbm, loc_sem.at[0])
    store_att.start()

    def back(k, key, value, r0, n, scale_row, last):
        keyT = key.T
        dk = jnp.zeros((n, HD), f32)
        dv = jnp.zeros((n, HD), f32)
        for p in range(4):
            c = cols(k * 4 + p, WIDE)
            d = doT[:, c]
            e = e_ref[r0 : r0 + n, c]
            ds = (e.astype(f32) * (dot(value, d) - st[4:5, c])).astype(bf16)
            sr = st[scale_row : scale_row + 1, c]
            dk += dot_nt(ds, (qT[:, c].astype(f32) * sr).astype(bf16))
            dv += dot_nt(e, (d.astype(f32) * sr).astype(bf16))
            g = dot(keyT, ds) * (sr * (adv * SCALE))
            if last:
                g = (g + dqT[:, c]).T
                for i in range(2):
                    dq_ref[:, cols((k * 4 + p) * 2 + i, HD)] = g[i * HD : (i + 1) * HD].astype(bf16)
            else:
                dqT[:, c] = g
        return (dk * (adv * SCALE)).astype(bf16), (dv * adv).astype(bf16)

    def back_rest(k, carry):
        key = jnp.concatenate([kv[0, 0, :, cols(k, HD)], kv[parent, 0, :, cols(k, HD)]], 0)
        value = jnp.concatenate([kv[0, 1, :, cols(k, HD)], kv[parent, 1, :, cols(k, HD)]], 0)
        dk, dv = back(k, key, value, TILE, 2 * TILE, 3, False)
        for i in range(2):
            mine[i, 0, :, cols(k, HD)] = dk[i * TILE : (i + 1) * TILE]
            mine[i, 1, :, cols(k, HD)] = dv[i * TILE : (i + 1) * TILE]
        return carry

    lax.fori_loop(0, KVH, back_rest, 0)

    swap = pltpu.make_async_remote_copy(
        src_ref=mine.at[pl.ds(0, 2)], dst_ref=theirs, send_sem=core_send.at[10],
        recv_sem=core_recv.at[10], device_id=dev_core, device_id_type=MESH,
    )
    swap.start()
    swap.wait_recv()

    parent_mark = jnp.where(has_parent, parent, -1)

    def part(yy, zz, start=0, size=HALF):
        place_ = segment(yy, zz)
        rows = pl.ds(pl.multiple_of(((zz % 4) % 2) * HALF + start, 16), size)
        place_f = place_.astype(f32)
        own_w = jnp.where(parent_mark == place_, 1.0, 0.0)
        mate_w = jnp.where(mate == place_f, 1.0, 0.0)
        root_w = jnp.where(place_ == 0, 1.0, 0.0)
        return (
            mine[1, :, rows].astype(f32) * own_w
            + theirs[1, :, rows].astype(f32) * mate_w[None]
            + (mine[0, :, rows].astype(f32) + theirs[0, :, rows].astype(f32)) * root_w
        )

    def ship(i, value, device, start=0, size=HALF):
        rows = pl.ds(start, size)
        outbox[i, :, rows] = value.astype(bf16)
        copy = pltpu.make_async_remote_copy(
            src_ref=outbox.at[i, :, rows], dst_ref=inbox.at[i, :, rows], send_sem=rs_send.at[i],
            recv_sem=rs_recv.at[i], device_id=device, device_id_type=MESH,
        )
        copy.start()
        return copy

    zero_step = [
        ship(0, part(1 - y, z + 2, a0, an), dev_up, a0, an),
        ship(1, part(1 - y, z + 2, b0, bn), dev_down, b0, bn),
        ship(2, part(1 - y, z + 2, c0, cn), dev_y, c0, cn),
    ]

    def back_own(k, carry):
        dk, dv = back(k, kv[seg, 0, :, cols(k, HD)], kv[seg, 1, :, cols(k, HD)], 0, TILE, 2, True)
        mine[2, 0, :, cols(k, HD)] = dk
        mine[2, 1, :, cols(k, HD)] = dv
        return carry

    lax.fori_loop(0, 2, back_own, 0)

    def got(i, start=0, size=HALF):
        return inbox[i, :, pl.ds(start, size)].astype(f32)

    for copy in zero_step:
        copy.wait_recv()

    def padded(yy, zz, i, start, size):
        pieces = []
        if start > 0:
            pieces.append(part(yy, zz, 0, start))
        pieces.append(part(yy, zz, start, size) + got(i, start, size))
        if start + size < HALF:
            pieces.append(part(yy, zz, start + size, HALF - start - size))
        return jnp.concatenate(pieces, 1)

    one_step = [
        ship(3, padded(y, z + 2, 2, c0, cn), dev_up),
        ship(4, padded(1 - y, z + 3, 1, b0, bn), dev_down),
        ship(5, padded(1 - y, z + 1, 0, a0, an), dev_y),
    ]
    lax.fori_loop(2, KVH, back_own, 0)
    store_dq = pltpu.make_async_copy(dq_ref, dq_hbm, loc_sem.at[1])
    store_dq.start()
    for copy in one_step:
        copy.wait_recv()

    def own_part(zz):
        zz = zz % 4
        w = jnp.where(zz // 2 == z // 2, 1.0, 0.0)
        return mine[2, :, pl.ds(pl.multiple_of((zz % 2) * HALF, HALF), HALF)].astype(f32) * w

    two_step = [
        ship(6, part(y, z + 1) + got(3) + got(5) + own_part(z + 1), dev_up),
        ship(7, part(y, z + 3) + own_part(z + 3), dev_down),
        ship(8, part(1 - y, z) + got(4), dev_y),
    ]
    final = part(y, z) + own_part(z)
    for copy in two_step:
        copy.wait_recv()
    final = final + got(6) + got(7) + got(8)
    gk_ref[...] = final[0].astype(bf16)
    gv_ref[...] = final[1].astype(bf16)
    swap.wait_send()
    for copy in zero_step + one_step + two_step:
        copy.wait_send()
    store_att.wait()
    store_dq.wait()


def body(queries, keys, values, d_out, lengths, ancestors, rewards, pruned, branch_group):
    hbm = pl.BlockSpec(memory_space=pl.ANY)
    smem = pl.BlockSpec(memory_space=pltpu.SMEM)
    vmem = pl.BlockSpec(memory_space=pltpu.VMEM)
    dma = pltpu.SemaphoreType.DMA
    att, dq, gk, gv, adv = pl.pallas_call(
        kernel,
        out_shape=(
            jax.ShapeDtypeStruct((HALF, H * HD), bf16),
            jax.ShapeDtypeStruct((HALF, H * HD), bf16),
            jax.ShapeDtypeStruct((HALF, KVH * HD), bf16),
            jax.ShapeDtypeStruct((HALF, KVH * HD), bf16),
            jax.ShapeDtypeStruct((1, 128), f32),
        ),
        in_specs=[hbm] * 4 + [smem] * 5,
        out_specs=(hbm, hbm, vmem, vmem, vmem),
        scratch_shapes=[
            pltpu.VMEM((HALF, H * HD), bf16),
            pltpu.VMEM((HALF, H * HD), bf16),
            pltpu.VMEM((HALF, H * HD), bf16),
            pltpu.VMEM((HALF, H * HD), bf16),
            pltpu.VMEM((TREE, 2, TILE, KVH * HD), bf16),
            pltpu.VMEM((HD, H * HALF), bf16),
            pltpu.VMEM((HD, H * HALF), bf16),
            pltpu.VMEM((3 * TILE, H * HALF), bf16),
            pltpu.VMEM((HD, H * HALF), f32),
            pltpu.VMEM((HD, H * HALF), f32),
            pltpu.VMEM((8, H * HALF), f32),
            pltpu.VMEM((2, TILE, HALF), f32),
            pltpu.VMEM((8, 8, 128), f32),
            pltpu.VMEM((8, 8, 128), f32),
            pltpu.VMEM((8, 128), f32),
            pltpu.VMEM((3, 2, TILE, KVH * HD), bf16),
            pltpu.VMEM((2, 2, TILE, KVH * HD), bf16),
            pltpu.VMEM((9, 2, HALF, KVH * HD), bf16),
            pltpu.VMEM((9, 2, HALF, KVH * HD), bf16),
            dma((4,)),
            dma((9,)),
            dma((9,)),
            dma((11,)),
            dma((11,)),
            dma((15,)),
            dma((15,)),
            dma((9,)),
            dma((9,)),
        ],
        compiler_params=pltpu.CompilerParams(
            collective_id=0, has_side_effects=True, vmem_limit_bytes=56 << 20
        ),
        name="tree_attention",
    )(queries, keys, values, d_out, lengths, ancestors, rewards, pruned, branch_group)
    return att, dq, gk, gv, adv[0, :1]


def solution(mesh):
    rows = P(("ctx", "tp"), None)
    in_specs = (rows, rows, rows, rows, P(), P("ctx", None), P("ctx"), P("ctx"), P("ctx"))
    out_specs = (rows, rows, rows, rows, P("ctx"))
    return jax.shard_map(body, mesh=mesh, in_specs=in_specs, out_specs=out_specs, check_vma=False)
```

profile of v0, /device:TPU:8, one launch (start us, length us, event | category | flops | bytes accessed | tf_op | source)
XLA Modules:
  0.0 76.8 jit_solution(12813283716082577541)
XLA Ops:
  2.6 68.1 %tree_attention.1 = (bf16[128,4096]{1,0:T(8,128)(2,1)}, bf16[128,4096]{1,0:T(8,128)(2,1)}, bf16[128,512]{1,0:T(8,128)(2,1)}, bf16[128,512]{1,0:T(8,128)(2,1)}, f32[1,128]{1,0:T(1,128)}) custom-call(bf16[128,4096]{1,0:T(8,128)(2,1)} %q_hbm.1, bf16[128,512]{1,0:T(8,128)(2,1)} %k_hbm.1, bf16[128,512]{1,0:T(8,128)(2,1)} %v_hbm.1, bf16[128,4096]{1,0:T(8,128)(2,1)} %do_hbm.1, ...), custom_call_target="tpu_custom_call" | custom-call | tf_op jit(solution)/shard_map/tree_attention/pallas_call | solution.py:404
  70.6 0.0 copy-start
  70.7 2.4 %copy.22 = bf16[128,4096]{1,0:T(8,128)(2,1)} copy(bf16[128,4096]{1,0:T(8,128)(2,1)} %get-tuple-element.20) | data formatting | bytes 2097152
  73.0 0.0 copy-done
  73.0 0.0 copy-start.2
  73.0 1.0 %copy.23 = bf16[128,4096]{1,0:T(8,128)(2,1)} copy(bf16[128,4096]{1,0:T(8,128)(2,1)S(1)} %copy-done) | data formatting | bytes 2097152
  74.0 0.1 copy-done.2
  74.1 0.0 copy-start.1
  74.1 0.7 copy.24
  74.7 0.3 copy-done.1
  75.0 0.0 copy-start.3
  75.0 0.7 copy.25
  75.7 0.0 copy-done.3
Async XLA Ops:
  70.6 2.4 %copy-start = (bf16[128,4096]{1,0:T(8,128)(2,1)S(1)}, bf16[128,4096]{1,0:T(8,128)(2,1)}, u32[]{:S(2)}) copy-start(bf16[128,4096]{1,0:T(8,128)(2,1)} %get-tuple-element.21) | copy-start | bytes 3145732
  73.0 1.0 %copy-start.2 = (bf16[128,512]{1,0:T(8,128)(2,1)S(1)}, bf16[128,512]{1,0:T(8,128)(2,1)}, u32[]{:S(2)}) copy-start(bf16[128,512]{1,0:T(8,128)(2,1)} %get-tuple-element.22) | copy-start | bytes 393220
  74.1 1.0 %copy-start.1 = (bf16[128,512]{1,0:T(8,128)(2,1)S(1)}, bf16[128,512]{1,0:T(8,128)(2,1)}, u32[]{:S(2)}) copy-start(bf16[128,512]{1,0:T(8,128)(2,1)} %get-tuple-element.23) | copy-start | bytes 393220
  75.0 0.7 copy-start.3
where the time goes:
time: 78 us; the launch traced here: 76.8 us
  Pallas kernels  68.1 us (87%)
  local copies, waits for them, and re-layouts  5.01 us (6%)
  between operations  3.76 us (5%)
    pallas_call x1, Pallas kernels, body(): pl.pallas_call(kernel, out_shape=(jax.ShapeDtypeStruct((HALF, H * HD), bf...  68.1 us
    unnamed x12, local copies, waits for them, and re-layouts  5.01 us

commit v1 on v0

v1 whole, which is shorter than its diff:
```python
import jax
import jax.numpy as jnp
from jax import lax
from jax.experimental import pallas as pl
from jax.experimental.pallas import tpu as pltpu
from jax.sharding import PartitionSpec as P

H = 32
KVH = 4
HD = 128
TILE = 256
HALF = 128
TREE = 8
GROUPS = 8
WIDE = 1024
MESH = pl.DeviceIdType.MESH
SCALE = HD**-0.5
LOG2 = SCALE * 1.4426950408889634
NEG = -1e30
f32 = jnp.float32
bf16 = jnp.bfloat16
NT = (((1,), (1,)), ((), ()))
SPLIT = 80


def cols(index, size):
    return pl.ds(pl.multiple_of(index * size, size), size)


def dot(a, b):
    return jnp.dot(a, b, preferred_element_type=f32)


def dot_nt(a, b):
    return lax.dot_general(a, b, NT, preferred_element_type=f32)


def kernel(
    q_hbm, k_hbm, v_hbm, do_hbm, len_hbm, anc_hbm, rew_hbm, pru_hbm, grp_hbm,
    att_hbm, dq_hbm, gk_hbm, gv_hbm, adv_hbm,
    q_ref, do_ref, att_ref, dq_ref, gk_ref, gv_ref, adv_ref,
    len_ref, anc_ref, rew_ref, pru_ref, grp_ref,
    kv, qT, doT, bias, near, far, mine, theirs, inbox, outbox,
    loc_sem, out_sem, ag_send, ag_recv, core_send, core_recv, st_send, st_recv, rs_send, rs_recv,
):
    ctx = lax.axis_index("ctx")
    tp = lax.axis_index("tp")
    tree = ctx // TREE
    seg = ctx % TREE
    core = ctx % 2
    z = ((ctx // 2) % 2) * 2 + tp
    y = (ctx // 4) % 2
    first = tree * TREE

    def place(yy, zz, cc):
        zz = zz % 4
        return first + yy * 4 + (zz // 2) * 2 + cc, zz % 2

    dev_core = place(y, z, 1 - core)
    dev_up = place(y, z + 1, core)
    dev_down = place(y, z + 3, core)
    dev_far = place(y, z + 2, core)
    dev_y = place(1 - y, z, core)
    kin = [(first + (seg + i) % TREE, tp) for i in range(1, TREE)]
    others = [(((tree + i) % 8) * TREE + seg, tp) for i in range(1, 8)]

    barrier = pltpu.get_barrier_semaphore()
    for device in kin + [dev_up, dev_down] + others:
        pl.semaphore_signal(barrier, inc=1, device_id=device, device_id_type=MESH)

    small = [
        pltpu.make_async_copy(a, b, loc_sem.at[i])
        for i, (a, b) in enumerate(
            zip(
                (len_hbm, anc_hbm, rew_hbm, pru_hbm, grp_hbm),
                (len_ref, anc_ref, rew_ref, pru_ref, grp_ref),
            )
        )
    ]
    rows_here = pl.ds(tp * HALF, HALF)
    large = [
        pltpu.make_async_copy(q_hbm, q_ref, loc_sem.at[5]),
        pltpu.make_async_copy(do_hbm, do_ref, loc_sem.at[6]),
    ]
    own_kv = []
    for h in range(KVH):
        for i, ref in enumerate((k_hbm, v_hbm)):
            own_kv.append(
                pltpu.make_async_copy(
                    ref.at[:, pl.ds(h * HD, HD)],
                    kv.at[h, core, y * 2 + z // 2, i, rows_here],
                    loc_sem.at[7 + 2 * h + i],
                )
            )
    for copy in small + large + own_kv:
        copy.start()
    for copy in small:
        copy.wait()

    lane = lax.broadcasted_iota(jnp.int32, (8, 128), 1)
    row = lax.broadcasted_iota(jnp.int32, (8, 128), 0)
    reward = rew_ref[0]
    living = 1.0 - pru_ref[0].astype(f32)
    belongs = lane == grp_ref[0]
    parent = jnp.int32(0)
    for o in range(1, TREE):
        parent = parent + jnp.where(o < seg, anc_ref[0, o - 1] * (seg - o), 0)
    has_parent = parent > 0
    terms = jnp.where(
        row == 0, living, jnp.where(row == 1, living * reward, living * reward * reward)
    )
    near[0] = jnp.where(
        row < 3, jnp.where(belongs, terms, 0.0), jnp.where(has_parent, parent, -1).astype(f32)
    )

    own_len = len_ref[ctx]
    par_len = jnp.where(has_parent, len_ref[first + parent], 0)
    u = lax.broadcasted_iota(jnp.int32, (TILE, HALF), 0)
    t = lax.broadcasted_iota(jnp.int32, (TILE, HALF), 1) + tp * HALF
    bias[0] = jnp.where((u <= t) & (u < own_len), 0.0, NEG)
    bias[1] = jnp.where(u < par_len, 0.0, NEG)
    root_off = jnp.where(seg > 0, 0.0, -NEG)
    slot = lax.broadcasted_iota(jnp.int32, (1, WIDE), 1) % HALF + tp * HALF
    seen = slot < own_len
    for copy in large:
        copy.wait()

    def turn(h, carry):
        qT[:, cols(h, HD)] = q_ref[:, cols(h, HD)].T
        doT[:, cols(h, HD)] = do_ref[:, cols(h, HD)].T
        return carry

    lax.fori_loop(0, H, turn, 0, unroll=4)
    for copy in own_kv:
        copy.wait()
    pl.semaphore_wait(barrier, 16)

    def remote(src, dst, device, sends, recvs, i):
        return pltpu.make_async_remote_copy(
            src_ref=src, dst_ref=dst, send_sem=sends.at[i], recv_sem=recvs.at[i],
            device_id=device, device_id_type=MESH,
        )

    def start(copies):
        for copy in copies:
            copy.start()

    def receive(copies):
        for copy in copies:
            copy.wait_recv()

    def block(h, yy, zz, begin=0, size=HALF):
        zz = zz % 4
        return kv.at[
            h, core, yy * 2 + zz // 2, :, pl.ds(pl.multiple_of((zz % 2) * HALF + begin, 16), size)
        ]

    def gather(h, pieces, base):
        return [
            remote(ref, ref, device, ag_send, ag_recv, h * 9 + base + i)
            for i, (ref, device) in enumerate(pieces)
        ]

    def gather_one(h):
        here = block(h, y, z)
        return gather(h, [(here, dev_up), (here, dev_down), (here, dev_y), (here, dev_far)], 0)

    def gather_two(h):
        over = block(h, 1 - y, z, 0, SPLIT)
        rest = HALF - SPLIT
        return gather(
            h,
            [
                (over, dev_up),
                (over, dev_down),
                (block(h, y, z + 1, SPLIT, rest), dev_y),
                (block(h, y, z + 3, SPLIT, rest), dev_y),
                (block(h, y, z + 2), dev_y),
            ],
            4,
        )

    def share(h, yy, i):
        ref = kv.at[h, core, pl.ds(yy * 2, 2)]
        return [remote(ref, ref, dev_core, core_send, core_recv, h * 3 + i)]

    def share_one(h):
        return share(h, y, 0)

    def share_two(h):
        return share(h, 1 - y, 1)

    notes = [
        remote(near.at[0], near.at[i], kin[i - 1], st_send, st_recv, i) for i in range(1, TREE)
    ]
    more = [
        remote(far.at[0], far.at[i], others[i - 1], st_send, st_recv, 7 + i) for i in range(1, 8)
    ]

    start(gather_one(0))
    start(notes)
    start(gather_one(1))
    receive(gather_one(0))
    start(gather_two(0) + share_one(0) + gather_one(2))
    receive(notes)
    summed = near[0]
    for i in range(1, TREE):
        summed = summed + near[i]
    far[0] = summed
    mate = jnp.where(core == 0, near[7], near[1])[3:4, 0:1]
    start(more)
    receive(gather_one(1))
    start(gather_two(1) + share_one(1) + gather_one(3))
    receive(gather_two(0))
    start(share_two(0))
    receive(more)
    summed = far[0]
    for i in range(1, 8):
        summed = summed + far[i]
    members = jnp.maximum(summed[0:1], 1.0)
    average = summed[1:2] / members
    spread = jnp.sqrt(jnp.maximum(summed[2:3] / members - average * average, 0.0))
    here = belongs[0:1]
    adv = (
        living
        * (reward - jnp.sum(jnp.where(here, average, 0.0), 1, keepdims=True))
        / jnp.sum(jnp.where(here, jnp.maximum(spread, 1.0), 0.0), 1, keepdims=True)
    )
    adv_ref[...] = jnp.broadcast_to(adv, (8, 128))
    store_adv = pltpu.make_async_copy(adv_ref, adv_hbm, out_sem.at[0])
    store_adv.start()

    def swap(h):
        return [
            remote(
                mine.at[h, pl.ds(0, 2)], theirs.at[h], dev_core, core_send, core_recv, h * 3 + 2
            )
        ]

    parent_mark = jnp.where(has_parent, parent, -1)

    def part(h, yy, zz, begin=0, size=HALF):
        zz = zz % 4
        target = yy * 4 + (zz // 2) * 2 + core
        rows = pl.ds(pl.multiple_of((zz % 2) * HALF + begin, 16), size)
        own_w = jnp.where(parent_mark == target, 1.0, 0.0)
        mate_w = jnp.where(mate == target.astype(f32), 1.0, 0.0)
        root_w = jnp.where(target == 0, 1.0, 0.0)
        return (
            mine[h, 1, :, rows].astype(f32) * own_w
            + theirs[h, 1, :, rows].astype(f32) * mate_w[None]
            + (mine[h, 0, :, rows].astype(f32) + theirs[h, 0, :, rows].astype(f32)) * root_w
        )

    def own_part(h, zz):
        zz = zz % 4
        w = jnp.where(zz // 2 == z // 2, 1.0, 0.0)
        rows = pl.ds(pl.multiple_of((zz % 2) * HALF, HALF), HALF)
        return mine[h, 2, :, rows].astype(f32) * w

    low = pl.ds(0, SPLIT)
    high = pl.ds(SPLIT, HALF - SPLIT)
    whole = pl.ds(0, HALF)

    def ship(h, i, rows, device):
        return remote(
            outbox.at[h, i, :, rows], inbox.at[h, i, :, rows], device, rs_send, rs_recv, h * 9 + i
        )

    def reduce_one(h):
        return [
            ship(h, 0, low, dev_up),
            ship(h, 1, low, dev_down),
            ship(h, 2, high, dev_y),
            ship(h, 3, high, dev_y),
            ship(h, 4, whole, dev_y),
        ]

    def reduce_two(h):
        return [
            ship(h, 5, whole, dev_y),
            ship(h, 6, whole, dev_up),
            ship(h, 7, whole, dev_down),
            ship(h, 8, whole, dev_far),
        ]

    def fill_one(h):
        up = part(h, 1 - y, z + 1).astype(bf16)
        down = part(h, 1 - y, z + 3).astype(bf16)
        outbox[h, 0, :, low] = up[:, :SPLIT]
        outbox[h, 1, :, low] = down[:, :SPLIT]
        outbox[h, 2, :, high] = up[:, SPLIT:]
        outbox[h, 3, :, high] = down[:, SPLIT:]
        outbox[h, 4] = part(h, 1 - y, z + 2).astype(bf16)

    def got(h, i, rows=whole):
        return inbox[h, i, :, rows].astype(f32)

    def fill_two(h):
        over = part(h, 1 - y, z)
        outbox[h, 5, :, low] = (over[:, :SPLIT] + got(h, 0, low) + got(h, 1, low)).astype(bf16)
        outbox[h, 5, :, high] = over[:, SPLIT:].astype(bf16)
        for i, zz in ((6, z + 1), (7, z + 3)):
            side = part(h, y, zz) + own_part(h, zz)
            outbox[h, i, :, low] = side[:, :SPLIT].astype(bf16)
            outbox[h, i, :, high] = (side[:, SPLIT:] + got(h, i - 4, high)).astype(bf16)
        outbox[h, 8] = (part(h, y, z + 2) + got(h, 4)).astype(bf16)

    def close(h):
        total = part(h, y, z) + own_part(h, z)
        for i in range(5, 9):
            total = total + got(h, i)
        gk_ref[:, cols(h, HD)] = total[0].astype(bf16)
        gv_ref[:, cols(h, HD)] = total[1].astype(bf16)

    def store(h, i):
        ref, out = ((att_ref, att_hbm), (dq_ref, dq_hbm))[i]
        c = cols(h, WIDE)
        return pltpu.make_async_copy(ref.at[:, c], out.at[:, c], out_sem.at[1 + 2 * h + i])

    def head(h, carry):
        receive(share_one(h) + share_two(h))
        c = cols(h, WIDE)

        @pl.when(h == 3)
        def _():
            receive(reduce_one(0))
            fill_two(0)
            start(reduce_two(0))

        def tiles(i):
            chosen = kv[h, 1, 0, i]
            for other in range(2, TREE - 1):
                chosen = jnp.where(parent == other, kv[h, other % 2, other // 2, i], chosen)
            return jnp.concatenate(
                [kv[h, core, y * 2 + z // 2, i], kv[h, 0, 0, i], chosen], 0
            )

        key = tiles(0)
        value = tiles(1)
        s = dot(key, qT[:, c])
        so = s[:TILE] + jnp.concatenate([bias[0]] * 8, 1)
        sr = s[TILE : 2 * TILE]
        sp = s[2 * TILE :] + jnp.concatenate([bias[1]] * 8, 1)
        m = (
            jnp.maximum(
                jnp.maximum(jnp.max(so, 0, keepdims=True), jnp.max(sp, 0, keepdims=True)),
                jnp.max(sr, 0, keepdims=True) - root_off,
            )
            * LOG2
        )
        eo = jnp.exp2(so * LOG2 - m)
        er = jnp.exp2(sr * LOG2 - (m + root_off))
        ep = jnp.exp2(sp * LOG2 - m)
        inv = jnp.where(seen, 1.0 / jnp.sum(eo + er + ep, 0, keepdims=True), 0.0)
        e = jnp.concatenate([eo, er, ep], 0).astype(bf16)
        o = dot(value.T, e) * inv
        d = doT[:, c]
        delta = jnp.sum(o * d.astype(f32), 0, keepdims=True)
        o = o.T
        for i in range(8):
            att_ref[:, cols(h * 8 + i, HD)] = o[i * HD : (i + 1) * HD].astype(bf16)
        store(h, 0).start()

        @pl.when(h < 2)
        def _():
            receive(gather_one(h + 2))
            start(gather_two(h + 2) + share_one(h + 2))

        @pl.when(h < 3)
        def _():
            receive(gather_two(h + 1))
            start(share_two(h + 1))

        @pl.when(h > 0)
        def _():
            receive(swap(h - 1))
            fill_one(h - 1)
            start(reduce_one(h - 1))

        ds = (e.astype(f32) * (dot(value, d) - delta)).astype(bf16)
        dk = dot_nt(ds, (qT[:, c].astype(f32) * inv).astype(bf16)) * (adv * SCALE)
        dv = dot_nt(e, (d.astype(f32) * inv).astype(bf16)) * adv
        for i, place_ in enumerate((2, 0, 1)):
            mine[h, place_, 0] = dk[i * TILE : (i + 1) * TILE].astype(bf16)
            mine[h, place_, 1] = dv[i * TILE : (i + 1) * TILE].astype(bf16)
        start(swap(h))
        g = (dot(key.T, ds) * (inv * (adv * SCALE))).T
        for i in range(8):
            dq_ref[:, cols(h * 8 + i, HD)] = g[i * HD : (i + 1) * HD].astype(bf16)
        store(h, 1).start()
        return carry

    lax.fori_loop(0, KVH, head, 0)

    def second(h):
        receive(reduce_one(h))
        fill_two(h)
        start(reduce_two(h))

    second(1)
    receive(swap(3))
    fill_one(3)
    start(reduce_one(3))
    second(2)
    receive(reduce_two(0))
    close(0)
    second(3)
    for h in range(1, KVH):
        receive(reduce_two(h))
        close(h)
    stores = [
        pltpu.make_async_copy(gk_ref, gk_hbm, out_sem.at[9]),
        pltpu.make_async_copy(gv_ref, gv_hbm, out_sem.at[10]),
    ]
    start(stores)
    for copy in stores + [store_adv] + [store(h, i) for h in range(KVH) for i in range(2)]:
        copy.wait()
    for copy in notes + more:
        copy.wait_send()

    def drain(h, carry):
        sent = gather_one(h) + gather_two(h) + share_one(h) + share_two(h)
        for copy in sent + swap(h) + reduce_one(h) + reduce_two(h):
            copy.wait_send()
        return carry

    lax.fori_loop(0, KVH, drain, 0)


def finish(*refs):
    ins, outs, bufs, adv_out = refs[:5], refs[5:9], refs[10:15], refs[9]
    arrive, leave = refs[15], refs[16]
    loads = [pltpu.make_async_copy(ins[i], bufs[i], arrive.at[i]) for i in range(5)]
    stores = [pltpu.make_async_copy(bufs[i], outs[i], leave.at[i]) for i in range(4)]
    for copy in loads:
        copy.start()
    for load, copy in zip(loads, stores):
        load.wait()
        copy.start()
    loads[4].wait()
    adv_out[0] = bufs[4][0, 0]
    for copy in stores:
        copy.wait()


def body(queries, keys, values, d_out, lengths, ancestors, rewards, pruned, branch_group):
    hbm = pl.BlockSpec(memory_space=pl.ANY)
    dma = pltpu.SemaphoreType.DMA
    wide = jax.ShapeDtypeStruct((HALF, H * HD), bf16)
    narrow = jax.ShapeDtypeStruct((HALF, KVH * HD), bf16)
    i32 = jnp.int32
    results = pl.pallas_call(
        kernel,
        out_shape=(wide, wide, narrow, narrow, jax.ShapeDtypeStruct((8, 128), f32)),
        in_specs=[hbm] * 9,
        out_specs=(hbm,) * 5,
        scratch_shapes=[
            pltpu.VMEM((HALF, H * HD), bf16),
            pltpu.VMEM((HALF, H * HD), bf16),
            pltpu.VMEM((HALF, H * HD), bf16),
            pltpu.VMEM((HALF, H * HD), bf16),
            pltpu.VMEM((HALF, KVH * HD), bf16),
            pltpu.VMEM((HALF, KVH * HD), bf16),
            pltpu.VMEM((8, 128), f32),
            pltpu.SMEM(lengths.shape, i32),
            pltpu.SMEM(ancestors.shape, i32),
            pltpu.SMEM((1,), f32),
            pltpu.SMEM((1,), i32),
            pltpu.SMEM((1,), i32),
            pltpu.VMEM((KVH, 2, 4, 2, TILE, HD), bf16),
            pltpu.VMEM((HD, H * HALF), bf16),
            pltpu.VMEM((HD, H * HALF), bf16),
            pltpu.VMEM((2, TILE, HALF), f32),
            pltpu.VMEM((8, 8, 128), f32),
            pltpu.VMEM((8, 8, 128), f32),
            pltpu.VMEM((KVH, 3, 2, TILE, HD), bf16),
            pltpu.VMEM((KVH, 2, 2, TILE, HD), bf16),
            pltpu.VMEM((KVH, 9, 2, HALF, HD), bf16),
            pltpu.VMEM((KVH, 9, 2, HALF, HD), bf16),
            dma((15,)),
            dma((11,)),
            dma((36,)),
            dma((36,)),
            dma((12,)),
            dma((12,)),
            dma((15,)),
            dma((15,)),
            dma((36,)),
            dma((36,)),
        ],
        compiler_params=pltpu.CompilerParams(
            collective_id=0, has_side_effects=True, vmem_limit_bytes=56 << 20
        ),
        name="tree_attention",
    )(queries, keys, values, d_out, lengths, ancestors, rewards, pruned, branch_group)
    return pl.pallas_call(
        finish,
        out_shape=(wide, wide, narrow, narrow, jax.ShapeDtypeStruct((1,), f32)),
        in_specs=[hbm] * 5,
        out_specs=(hbm,) * 4 + (pl.BlockSpec(memory_space=pltpu.SMEM),),
        scratch_shapes=[pltpu.VMEM(a.shape, a.dtype) for a in results] + [dma((5,)), dma((4,))],
        name="finish",
    )(*results)


def solution(mesh):
    rows = P(("ctx", "tp"), None)
    in_specs = (rows, rows, rows, rows, P(), P("ctx", None), P("ctx"), P("ctx"), P("ctx"))
    out_specs = (rows, rows, rows, rows, P("ctx"))
    return jax.shard_map(body, mesh=mesh, in_specs=in_specs, out_specs=out_specs, check_vma=False)
```

time: 78 us -> 58.6 us (0.75)
  the two profiles are of different devices: /device:TPU:8 before, /device:TPU:0 now
where the time goes in v1:
time: 58.6 us; the launch traced here: 58.4 us
  Pallas kernels  55.9 us (95%)
  between operations  2.58 us (4%)
    pallas_call x1, Pallas kernels, body(): pl.pallas_call(kernel, out_shape=(wide, wide, narrow, narrow, jax.ShapeDt...  52.6 us
    pallas_call x1, Pallas kernels, body(): pl.pallas_call(finish, out_shape=(wide, wide, narrow, narrow, jax.ShapeDt...  3.21 us

profile of v1, /device:TPU:0, one launch (start us, length us, event | category | flops | bytes accessed | tf_op | source)
XLA Modules:
  0.0 58.4 jit_solution(2230368853481724246)
XLA Ops:
  2.6 52.6 %tree_attention.1 = (bf16[128,4096]{1,0:T(8,128)(2,1)}, bf16[128,4096]{1,0:T(8,128)(2,1)}, bf16[128,512]{1,0:T(8,128)(2,1)}, bf16[128,512]{1,0:T(8,128)(2,1)}, f32[8,128]{1,0:T(8,128)}) custom-call(bf16[128,4096]{1,0:T(8,128)(2,1)} %q_hbm.1, bf16[128,512]{1,0:T(8,128)(2,1)} %k_hbm.1, bf16[128,512]{1,0:T(8,128)(2,1)} %v_hbm.1, bf16[128,4096]{1,0:T(8,128)(2,1)} %do_hbm.1, ...), custom_call_target="tpu_custom_call" | custom-call | tf_op jit(solution)/shard_map/tree_attention/pallas_call | solution.py:453
  55.2 3.2 %finish.1 = (bf16[128,4096]{1,0:T(8,128)(2,1)}, bf16[128,4096]{1,0:T(8,128)(2,1)}, bf16[128,512]{1,0:T(8,128)(2,1)}, bf16[128,512]{1,0:T(8,128)(2,1)}, f32[1]{0:T(128)}) custom-call(bf16[128,4096]{1,0:T(8,128)(2,1)} %get-tuple-element.10.refs_0_, bf16[128,4096]{1,0:T(8,128)(2,1)} %get-tuple-element.11.refs_1_, bf16[128,512]{1,0:T(8,128)(2,1)} %get-tuple-element.12.refs_2_, ...), custom_call_target="tpu_custom_call" | custom-call | tf_op jit(solution)/shard_map/finish/pallas_call | solution.py:497

commit v2 on v1

--- a/solution.py
+++ b/solution.py
@@ -20,7 +20,7 @@
 f32 = jnp.float32
 bf16 = jnp.bfloat16
 NT = (((1,), (1,)), ((), ()))
-SPLIT = 80
+SPLIT = 64
 
 
 def cols(index, size):
@@ -41,7 +41,7 @@
     q_ref, do_ref, att_ref, dq_ref, gk_ref, gv_ref, adv_ref,
     len_ref, anc_ref, rew_ref, pru_ref, grp_ref,
     kv, qT, doT, bias, near, far, mine, theirs, inbox, outbox,
-    loc_sem, out_sem, ag_send, ag_recv, core_send, core_recv, st_send, st_recv, rs_send, rs_recv,
+    loc_sem, ag_send, ag_recv, core_send, core_recv, st_send, st_recv, rs_recv,
 ):
     ctx = lax.axis_index("ctx")
     tp = lax.axis_index("tp")
@@ -57,15 +57,17 @@
         return first + yy * 4 + (zz // 2) * 2 + cc, zz % 2
 
     dev_core = place(y, z, 1 - core)
-    dev_up = place(y, z + 1, core)
-    dev_down = place(y, z + 3, core)
+    pair = z + 1 - 2 * (z % 2)
+    side = z + 3 + 2 * (z % 2)
+    dev_pair = place(y, pair, core)
+    dev_side = place(y, side, core)
     dev_far = place(y, z + 2, core)
     dev_y = place(1 - y, z, core)
     kin = [(first + (seg + i) % TREE, tp) for i in range(1, TREE)]
     others = [(((tree + i) % 8) * TREE + seg, tp) for i in range(1, 8)]
 
     barrier = pltpu.get_barrier_semaphore()
-    for device in kin + [dev_up, dev_down] + others:
+    for device in kin + [dev_pair, dev_side] + others:
         pl.semaphore_signal(barrier, inc=1, device_id=device, device_id_type=MESH)
 
     small = [
@@ -113,6 +115,104 @@
         row < 3, jnp.where(belongs, terms, 0.0), jnp.where(has_parent, parent, -1).astype(f32)
     )
 
+    for copy in own_kv:
+        copy.wait()
+    pl.semaphore_wait(barrier, 16)
+
+    def remote(src, dst, device, sends, recvs, i):
+        return pltpu.make_async_remote_copy(
+            src_ref=src, dst_ref=dst, send_sem=sends.at[i], recv_sem=recvs.at[i],
+            device_id=device, device_id_type=MESH,
+        )
+
+    def act(method, moves, which):
+        for move in moves:
+            operation = getattr(move[0], method)
+            if move[which] is None:
+                operation()
+            else:
+                pl.when(move[which])(operation)
+
+    def start(moves):
+        act("start", moves, 1)
+
+    def receive(moves):
+        act("wait_recv", moves, 2)
+
+    def sent(moves):
+        act("wait_send", moves, 1)
+
+    lower = y == 0
+    upper = y == 1
+
+    def block(h, yy, zz, begin=0, size=HALF):
+        zz = zz % 4
+        return kv.at[
+            h, core, yy * 2 + zz // 2, :, pl.ds(pl.multiple_of((zz % 2) * HALF + begin, 16), size)
+        ]
+
+    def gather(h, pieces, base):
+        return [
+            (remote(ref, ref, device, ag_send, ag_recv, h * 8 + base + i), sends, gets)
+            for i, (ref, device, sends, gets) in enumerate(pieces)
+        ]
+
+    def gather_one(h):
+        here = block(h, y, z)
+        return gather(
+            h,
+            [
+                (here, dev_pair, None, None),
+                (here, dev_side, lower | (z < 2), lower | (z >= 2)),
+                (here, dev_y, lower, upper),
+                (here, dev_far, lower | (z < 2), lower | (z >= 2)),
+            ],
+            0,
+        )
+
+    def gather_two(h):
+        rest = HALF - SPLIT
+        return gather(
+            h,
+            [
+                (block(h, 1 - y, z), dev_pair, upper, upper),
+                (block(h, 1 - y, z, 0, SPLIT), dev_side, upper, upper),
+                (block(h, y, side, SPLIT, rest), dev_y, lower, upper),
+                (block(h, y, z + 2), dev_y, lower, upper),
+            ],
+            4,
+        )
+
+    def share(h, yy, i, needed):
+        ref = kv.at[h, core, pl.ds(yy * 2, 2)]
+        return [(remote(ref, ref, dev_core, core_send, core_recv, h * 3 + i), needed, needed)]
+
+    def share_one(h):
+        return share(h, y, 0, None)
+
+    def share_two(h):
+        return share(h, 1 - y, 1, upper)
+
+    notes = [
+        (remote(near.at[0], near.at[i], kin[i - 1], st_send, st_recv, i), None, None)
+        for i in range(1, TREE)
+    ]
+    more = [
+        (
+            pltpu.make_async_remote_copy(
+                src_ref=far.at[0], dst_ref=far.at[i], send_sem=st_send.at[i],
+                recv_sem=st_recv.at[7 + i], device_id=others[i - 1], device_id_type=MESH,
+            ),
+            None,
+            None,
+        )
+        for i in range(1, 8)
+    ]
+
+    start(gather_one(0))
+    start(notes)
+    start(gather_one(1))
+
     own_len = len_ref[ctx]
     par_len = jnp.where(has_parent, len_ref[first + parent], 0)
     u = lax.broadcasted_iota(jnp.int32, (TILE, HALF), 0)
@@ -131,75 +231,7 @@
         return carry
 
     lax.fori_loop(0, H, turn, 0, unroll=4)
-    for copy in own_kv:
-        copy.wait()
-    pl.semaphore_wait(barrier, 16)
-
-    def remote(src, dst, device, sends, recvs, i):
-        return pltpu.make_async_remote_copy(
-            src_ref=src, dst_ref=dst, send_sem=sends.at[i], recv_sem=recvs.at[i],
-            device_id=device, device_id_type=MESH,
-        )
-
-    def start(copies):
-        for copy in copies:
-            copy.start()
-
-    def receive(copies):
-        for copy in copies:
-            copy.wait_recv()
-
-    def block(h, yy, zz, begin=0, size=HALF):
-        zz = zz % 4
-        return kv.at[
-            h, core, yy * 2 + zz // 2, :, pl.ds(pl.multiple_of((zz % 2) * HALF + begin, 16), size)
-        ]
-
-    def gather(h, pieces, base):
-        return [
-            remote(ref, ref, device, ag_send, ag_recv, h * 9 + base + i)
-            for i, (ref, device) in enumerate(pieces)
-        ]
-
-    def gather_one(h):
-        here = block(h, y, z)
-        return gather(h, [(here, dev_up), (here, dev_down), (here, dev_y), (here, dev_far)], 0)
-
-    def gather_two(h):
-        over = block(h, 1 - y, z, 0, SPLIT)
-        rest = HALF - SPLIT
-        return gather(
-            h,
-            [
-                (over, dev_up),
-                (over, dev_down),
-                (block(h, y, z + 1, SPLIT, rest), dev_y),
-                (block(h, y, z + 3, SPLIT, rest), dev_y),
-                (block(h, y, z + 2), dev_y),
-            ],
-            4,
-        )
-
-    def share(h, yy, i):
-        ref = kv.at[h, core, pl.ds(yy * 2, 2)]
-        return [remote(ref, ref, dev_core, core_send, core_recv, h * 3 + i)]
-
-    def share_one(h):
-        return share(h, y, 0)
-
-    def share_two(h):
-        return share(h, 1 - y, 1)
-
-    notes = [
-        remote(near.at[0], near.at[i], kin[i - 1], st_send, st_recv, i) for i in range(1, TREE)
-    ]
-    more = [
-        remote(far.at[0], far.at[i], others[i - 1], st_send, st_recv, 7 + i) for i in range(1, 8)
-    ]
-
-    start(gather_one(0))
-    start(notes)
-    start(gather_one(1))
+
     receive(gather_one(0))
     start(gather_two(0) + share_one(0) + gather_one(2))
     receive(notes)
@@ -208,6 +240,7 @@
         summed = summed + near[i]
     far[0] = summed
     mate = jnp.where(core == 0, near[7], near[1])[3:4, 0:1]
+    sent(notes)
     start(more)
     receive(gather_one(1))
     start(gather_two(1) + share_one(1) + gather_one(3))
@@ -227,15 +260,14 @@
         / jnp.sum(jnp.where(here, jnp.maximum(spread, 1.0), 0.0), 1, keepdims=True)
     )
     adv_ref[...] = jnp.broadcast_to(adv, (8, 128))
-    store_adv = pltpu.make_async_copy(adv_ref, adv_hbm, out_sem.at[0])
+    store_adv = pltpu.make_async_copy(adv_ref, adv_hbm, loc_sem.at[0])
     store_adv.start()
 
     def swap(h):
-        return [
-            remote(
-                mine.at[h, pl.ds(0, 2)], theirs.at[h], dev_core, core_send, core_recv, h * 3 + 2
-            )
-        ]
+        copy = remote(
+            mine.at[h, pl.ds(0, 2)], theirs.at[h], dev_core, core_send, core_recv, h * 3 + 2
+        )
+        return [(copy, None, None)]
 
     parent_mark = jnp.where(has_parent, parent, -1)
 
@@ -253,70 +285,88 @@
         )
 
     def own_part(h, zz):
-        zz = zz % 4
-        w = jnp.where(zz // 2 == z // 2, 1.0, 0.0)
         rows = pl.ds(pl.multiple_of((zz % 2) * HALF, HALF), HALF)
-        return mine[h, 2, :, rows].astype(f32) * w
+        return mine[h, 2, :, rows].astype(f32)
 
     low = pl.ds(0, SPLIT)
     high = pl.ds(SPLIT, HALF - SPLIT)
     whole = pl.ds(0, HALF)
 
-    def ship(h, i, rows, device):
-        return remote(
-            outbox.at[h, i, :, rows], inbox.at[h, i, :, rows], device, rs_send, rs_recv, h * 9 + i
-        )
+    def ship(h, i, rows, device, sends, gets):
+        copy = remote(
+            outbox.at[h, i, :, rows], inbox.at[h, i, :, rows], device, ag_send, rs_recv, h * 8 + i
+        )
+        return copy, sends, gets
 
     def reduce_one(h):
         return [
-            ship(h, 0, low, dev_up),
-            ship(h, 1, low, dev_down),
-            ship(h, 2, high, dev_y),
-            ship(h, 3, high, dev_y),
-            ship(h, 4, whole, dev_y),
+            ship(h, 0, whole, dev_pair, upper, upper),
+            ship(h, 1, low, dev_side, upper, upper),
+            ship(h, 2, high, dev_y, upper, lower),
+            ship(h, 3, whole, dev_y, upper, lower),
         ]
 
     def reduce_two(h):
         return [
-            ship(h, 5, whole, dev_y),
-            ship(h, 6, whole, dev_up),
-            ship(h, 7, whole, dev_down),
-            ship(h, 8, whole, dev_far),
+            ship(h, 4, whole, dev_y, upper, lower),
+            ship(h, 5, whole, dev_pair, None, None),
+            ship(h, 6, whole, dev_side, lower | (z >= 2), lower | (z < 2)),
+            ship(h, 7, whole, dev_far, lower | (z >= 2), lower | (z < 2)),
         ]
 
     def fill_one(h):
-        up = part(h, 1 - y, z + 1).astype(bf16)
-        down = part(h, 1 - y, z + 3).astype(bf16)
-        outbox[h, 0, :, low] = up[:, :SPLIT]
-        outbox[h, 1, :, low] = down[:, :SPLIT]
-        outbox[h, 2, :, high] = up[:, SPLIT:]
-        outbox[h, 3, :, high] = down[:, SPLIT:]
-        outbox[h, 4] = part(h, 1 - y, z + 2).astype(bf16)
+        @pl.when(upper)
+        def _():
+            outbox[h, 0] = part(h, 1 - y, pair).astype(bf16)
+            beside = part(h, 1 - y, side).astype(bf16)
+            outbox[h, 1, :, low] = beside[:, :SPLIT]
+            outbox[h, 2, :, high] = beside[:, SPLIT:]
+            outbox[h, 3] = part(h, 1 - y, z + 2).astype(bf16)
 
     def got(h, i, rows=whole):
         return inbox[h, i, :, rows].astype(f32)
 
     def fill_two(h):
-        over = part(h, 1 - y, z)
-        outbox[h, 5, :, low] = (over[:, :SPLIT] + got(h, 0, low) + got(h, 1, low)).astype(bf16)
-        outbox[h, 5, :, high] = over[:, SPLIT:].astype(bf16)
-        for i, zz in ((6, z + 1), (7, z + 3)):
-            side = part(h, y, zz) + own_part(h, zz)
-            outbox[h, i, :, low] = side[:, :SPLIT].astype(bf16)
-            outbox[h, i, :, high] = (side[:, SPLIT:] + got(h, i - 4, high)).astype(bf16)
-        outbox[h, 8] = (part(h, y, z + 2) + got(h, 4)).astype(bf16)
+        outbox[h, 5] = (part(h, y, pair) + own_part(h, pair)).astype(bf16)
+
+        @pl.when(upper)
+        def _():
+            over = part(h, 1 - y, z) + got(h, 0)
+            outbox[h, 4, :, low] = (over[:, :SPLIT] + got(h, 1, low)).astype(bf16)
+            outbox[h, 4, :, high] = over[:, SPLIT:].astype(bf16)
+            outbox[h, 6] = part(h, y, side).astype(bf16)
+            outbox[h, 7] = part(h, y, z + 2).astype(bf16)
+
+        @pl.when(lower)
+        def _():
+            beside = part(h, y, side)
+            outbox[h, 6, :, low] = beside[:, :SPLIT].astype(bf16)
+            outbox[h, 6, :, high] = (beside[:, SPLIT:] + got(h, 2, high)).astype(bf16)
+            outbox[h, 7] = (part(h, y, z + 2) + got(h, 3)).astype(bf16)
 
     def close(h):
         total = part(h, y, z) + own_part(h, z)
-        for i in range(5, 9):
-            total = total + got(h, i)
+        for i, (_, _, gets) in enumerate(reduce_two(h)):
+            term = got(h, 4 + i)
+            total = total + (term if gets is None else jnp.where(gets, term, 0.0))
         gk_ref[:, cols(h, HD)] = total[0].astype(bf16)
         gv_ref[:, cols(h, HD)] = total[1].astype(bf16)
+
+    def first_reduce(h):
+        receive(swap(h))
+        fill_one(h)
+        sent(gather_one(h) + gather_two(h))
+        start(reduce_one(h))
+
+    def second_reduce(h):
+        receive(reduce_one(h))
+        fill_two(h)
+        start(reduce_two(h))
 
     def store(h, i):
         ref, out = ((att_ref, att_hbm), (dq_ref, dq_hbm))[i]
         c = cols(h, WIDE)
-        return pltpu.make_async_copy(ref.at[:, c], out.at[:, c], out_sem.at[1 + 2 * h + i])
+        return pltpu.make_async_copy(ref.at[:, c], out.at[:, c], loc_sem.at[1 + 2 * h + i])
 
     def head(h, carry):
         receive(share_one(h) + share_two(h))
@@ -324,9 +374,7 @@
 
         @pl.when(h == 3)
         def _():
-            receive(reduce_one(0))
-            fill_two(0)
-            start(reduce_two(0))
+            second_reduce(0)
 
         def tiles(i):
             chosen = kv[h, 1, 0, i]
@@ -367,16 +415,14 @@
             receive(gather_one(h + 2))
             start(gather_two(h + 2) + share_one(h + 2))
 
+        @pl.when(h > 0)
+        def _():
+            first_reduce(h - 1)
+
         @pl.when(h < 3)
         def _():
             receive(gather_two(h + 1))
             start(share_two(h + 1))
-
-        @pl.when(h > 0)
-        def _():
-            receive(swap(h - 1))
-            fill_one(h - 1)
-            start(reduce_one(h - 1))
 
         ds = (e.astype(f32) * (dot(value, d) - delta)).astype(bf16)
         dk = dot_nt(ds, (qT[:, c].astype(f32) * inv).astype(bf16)) * (adv * SCALE)
@@ -393,36 +439,27 @@
 
     lax.fori_loop(0, KVH, head, 0)
 
-    def second(h):
-        receive(reduce_one(h))
-        fill_two(h)
-        start(reduce_two(h))
-
-    second(1)
-    receive(swap(3))
-    fill_one(3)
-    start(reduce_one(3))
-    second(2)
+    second_reduce(1)
+    first_reduce(3)
+    second_reduce(2)
     receive(reduce_two(0))
     close(0)
-    second(3)
+    second_reduce(3)
     for h in range(1, KVH):
         receive(reduce_two(h))
         close(h)
     stores = [
-        pltpu.make_async_copy(gk_ref, gk_hbm, out_sem.at[9]),
-        pltpu.make_async_copy(gv_ref, gv_hbm, out_sem.at[10]),
+        pltpu.make_async_copy(gk_ref, gk_hbm, loc_sem.at[9]),
+        pltpu.make_async_copy(gv_ref, gv_hbm, loc_sem.at[10]),
     ]
-    start(stores)
+    for copy in stores:
+        copy.start()
     for copy in stores + [store_adv] + [store(h, i) for h in range(KVH) for i in range(2)]:
         copy.wait()
-    for copy in notes + more:
-        copy.wait_send()
+    sent(more)
 
     def drain(h, carry):
-        sent = gather_one(h) + gather_two(h) + share_one(h) + share_two(h)
-        for copy in sent + swap(h) + reduce_one(h) + reduce_two(h):
-            copy.wait_send()
+        sent(share_one(h) + share_two(h) + swap(h) + reduce_one(h) + reduce_two(h))
         return carry
 
     lax.fori_loop(0, KVH, drain, 0)
@@ -476,18 +513,16 @@
             pltpu.VMEM((8, 8, 128), f32),
             pltpu.VMEM((KVH, 3, 2, TILE, HD), bf16),
             pltpu.VMEM((KVH, 2, 2, TILE, HD), bf16),
-            pltpu.VMEM((KVH, 9, 2, HALF, HD), bf16),
-            pltpu.VMEM((KVH, 9, 2, HALF, HD), bf16),
+            pltpu.VMEM((KVH, 8, 2, HALF, HD), bf16),
+            pltpu.VMEM((KVH, 8, 2, HALF, HD), bf16),
             dma((15,)),
-            dma((11,)),
-            dma((36,)),
-            dma((36,)),
+            dma((32,)),
+            dma((32,)),
             dma((12,)),
             dma((12,)),
+            dma((8,)),
             dma((15,)),
-            dma((15,)),
-            dma((36,)),
-            dma((36,)),
+            dma((32,)),
         ],
         compiler_params=pltpu.CompilerParams(
             collective_id=0, has_side_effects=True, vmem_limit_bytes=56 << 20

time: 58.6 us -> 55.6 us (0.949)
  the two profiles are of different devices: /device:TPU:0 before, /device:TPU:8 now
where the time goes in v2:
time: 55.6 us; the launch traced here: 55.4 us
  Pallas kernels  52.8 us (95%)
  between operations  2.58 us (5%)
    pallas_call x1, Pallas kernels, body(): pl.pallas_call(kernel, out_shape=(wide, wide, narrow, narrow, jax.ShapeDt...  49.6 us
    pallas_call x1, Pallas kernels, body(): pl.pallas_call(finish, out_shape=(wide, wide, narrow, narrow, jax.ShapeDt...  3.21 us

profile of v2, /device:TPU:8, one launch (start us, length us, event | category | flops | bytes accessed | tf_op | source)
XLA Modules:
  0.0 55.4 jit_solution(2526489616605562788)
XLA Ops:
  2.6 49.6 %tree_attention.1 = (bf16[128,4096]{1,0:T(8,128)(2,1)}, bf16[128,4096]{1,0:T(8,128)(2,1)}, bf16[128,512]{1,0:T(8,128)(2,1)}, bf16[128,512]{1,0:T(8,128)(2,1)}, f32[8,128]{1,0:T(8,128)}) custom-call(bf16[128,4096]{1,0:T(8,128)(2,1)} %q_hbm.1, bf16[128,512]{1,0:T(8,128)(2,1)} %k_hbm.1, bf16[128,512]{1,0:T(8,128)(2,1)} %v_hbm.1, bf16[128,4096]{1,0:T(8,128)(2,1)} %do_hbm.1, ...), custom_call_target="tpu_custom_call" | custom-call | tf_op jit(solution)/shard_map/tree_attention/pallas_call | solution.py:490
  52.2 3.2 %finish.1 = (bf16[128,4096]{1,0:T(8,128)(2,1)}, bf16[128,4096]{1,0:T(8,128)(2,1)}, bf16[128,512]{1,0:T(8,128)(2,1)}, bf16[128,512]{1,0:T(8,128)(2,1)}, f32[1]{0:T(128)}) custom-call(bf16[128,4096]{1,0:T(8,128)(2,1)} %get-tuple-element.10.refs_0_, bf16[128,4096]{1,0:T(8,128)(2,1)} %get-tuple-element.11.refs_1_, bf16[128,512]{1,0:T(8,128)(2,1)} %get-tuple-element.12.refs_2_, ...), custom_call_target="tpu_custom_call" | custom-call | tf_op jit(solution)/shard_map/finish/pallas_call | solution.py:532

commit v3 on v2

--- a/solution.py
+++ b/solution.py
@@ -445,37 +445,52 @@
     receive(reduce_two(0))
     close(0)
     second_reduce(3)
-    for h in range(1, KVH):
+    for h in (1, 2):
         receive(reduce_two(h))
         close(h)
+    sent(more)
+    store_adv.wait()
+
+    def drain(h, carry):
+        sent(share_one(h) + share_two(h) + swap(h) + reduce_one(h))
+        pl.when(h < 3)(lambda: sent(reduce_two(h)))
+        for i in range(2):
+            store(h, i).wait()
+        return carry
+
+    lax.fori_loop(0, KVH, drain, 0)
+    receive(reduce_two(3))
+    close(3)
     stores = [
         pltpu.make_async_copy(gk_ref, gk_hbm, loc_sem.at[9]),
         pltpu.make_async_copy(gv_ref, gv_hbm, loc_sem.at[10]),
     ]
     for copy in stores:
         copy.start()
-    for copy in stores + [store_adv] + [store(h, i) for h in range(KVH) for i in range(2)]:
+    sent(reduce_two(3))
+    for copy in stores:
         copy.wait()
-    sent(more)
-
-    def drain(h, carry):
-        sent(share_one(h) + share_two(h) + swap(h) + reduce_one(h) + reduce_two(h))
-        return carry
-
-    lax.fori_loop(0, KVH, drain, 0)
 
 
 def finish(*refs):
     ins, outs, bufs, adv_out = refs[:5], refs[5:9], refs[10:15], refs[9]
     arrive, leave = refs[15], refs[16]
-    loads = [pltpu.make_async_copy(ins[i], bufs[i], arrive.at[i]) for i in range(5)]
-    stores = [pltpu.make_async_copy(bufs[i], outs[i], leave.at[i]) for i in range(4)]
+    loads, stores = [], []
+    for i, pieces in enumerate((4, 4, 1, 1)):
+        size = HALF // pieces
+        for p in range(pieces):
+            rows = pl.ds(p * size, size)
+            n = len(loads)
+            loads.append(pltpu.make_async_copy(ins[i].at[rows], bufs[i].at[rows], arrive.at[n]))
+            stores.append(pltpu.make_async_copy(bufs[i].at[rows], outs[i].at[rows], leave.at[n]))
+    last = pltpu.make_async_copy(ins[4], bufs[4], arrive.at[10])
+    last.start()
     for copy in loads:
         copy.start()
     for load, copy in zip(loads, stores):
         load.wait()
         copy.start()
-    loads[4].wait()
+    last.wait()
     adv_out[0] = bufs[4][0, 0]
     for copy in stores:
         copy.wait()
@@ -534,7 +549,7 @@
         out_shape=(wide, wide, narrow, narrow, jax.ShapeDtypeStruct((1,), f32)),
         in_specs=[hbm] * 5,
         out_specs=(hbm,) * 4 + (pl.BlockSpec(memory_space=pltpu.SMEM),),
-        scratch_shapes=[pltpu.VMEM(a.shape, a.dtype) for a in results] + [dma((5,)), dma((4,))],
+        scratch_shapes=[pltpu.VMEM(a.shape, a.dtype) for a in results] + [dma((11,)), dma((10,))],
         name="finish",
     )(*results)
 

time: 55.6 us -> 55.4 us (level)
  no operation moved by 1% of the time
where the time goes in v3:
time: 55.4 us; the launch traced here: 55.2 us
  Pallas kernels  52.6 us (95%)
  between operations  2.58 us (5%)
    pallas_call x1, Pallas kernels, body(): pl.pallas_call(kernel, out_shape=(wide, wide, narrow, narrow, jax.ShapeDt...  49.5 us
    pallas_call x1, Pallas kernels, body(): pl.pallas_call(finish, out_shape=(wide, wide, narrow, narrow, jax.ShapeDt...  3.04 us

profile of v3, /device:TPU:8, one launch (start us, length us, event | category | flops | bytes accessed | tf_op | source)
XLA Modules:
  0.0 55.2 jit_solution(13824606001671578752)
XLA Ops:
  2.6 49.5 %tree_attention.1 = (bf16[128,4096]{1,0:T(8,128)(2,1)}, bf16[128,4096]{1,0:T(8,128)(2,1)}, bf16[128,512]{1,0:T(8,128)(2,1)}, bf16[128,512]{1,0:T(8,128)(2,1)}, f32[8,128]{1,0:T(8,128)}) custom-call(bf16[128,4096]{1,0:T(8,128)(2,1)} %q_hbm.1, bf16[128,512]{1,0:T(8,128)(2,1)} %k_hbm.1, bf16[128,512]{1,0:T(8,128)(2,1)} %v_hbm.1, bf16[128,4096]{1,0:T(8,128)(2,1)} %do_hbm.1, ...), custom_call_target="tpu_custom_call" | custom-call | tf_op jit(solution)/shard_map/tree_attention/pallas_call | solution.py:505
  52.1 3.0 %finish.1 = (bf16[128,4096]{1,0:T(8,128)(2,1)}, bf16[128,4096]{1,0:T(8,128)(2,1)}, bf16[128,512]{1,0:T(8,128)(2,1)}, bf16[128,512]{1,0:T(8,128)(2,1)}, f32[1]{0:T(128)}) custom-call(bf16[128,4096]{1,0:T(8,128)(2,1)} %get-tuple-element.10.refs_0_, bf16[128,4096]{1,0:T(8,128)(2,1)} %get-tuple-element.11.refs_1_, bf16[128,512]{1,0:T(8,128)(2,1)} %get-tuple-element.12.refs_2_, ...), custom_call_target="tpu_custom_call" | custom-call | tf_op jit(solution)/shard_map/finish/pallas_call | solution.py:547

commit v4 on v3

--- a/solution.py
+++ b/solution.py
@@ -439,8 +439,8 @@
 
     lax.fori_loop(0, KVH, head, 0)
 
+    first_reduce(3)
     second_reduce(1)
-    first_reduce(3)
     second_reduce(2)
     receive(reduce_two(0))
     close(0)

time: 55.4 us -> 56.4 us (1.018)
  Pallas kernels: 52.6 us -> 53.5 us
    pallas_call x1, Pallas kernels: 49.5 us -> 50.5 us  [body(): pl.pallas_call(kernel, out_shape=(wide, wide, narrow, narrow, jax.ShapeDt...]
where the time goes in v4:
time: 56.4 us; the launch traced here: 56.1 us
  Pallas kernels  53.5 us (95%)
  between operations  2.58 us (5%)
    pallas_call x1, Pallas kernels, body(): pl.pallas_call(kernel, out_shape=(wide, wide, narrow, narrow, jax.ShapeDt...  50.5 us
    pallas_call x1, Pallas kernels, body(): pl.pallas_call(finish, out_shape=(wide, wide, narrow, narrow, jax.ShapeDt...  3.04 us

profile of v4, /device:TPU:8, one launch (start us, length us, event | category | flops | bytes accessed | tf_op | source)
XLA Modules:
  0.0 56.1 jit_solution(2609519281758369372)
XLA Ops:
  2.6 50.5 %tree_attention.1 = (bf16[128,4096]{1,0:T(8,128)(2,1)}, bf16[128,4096]{1,0:T(8,128)(2,1)}, bf16[128,512]{1,0:T(8,128)(2,1)}, bf16[128,512]{1,0:T(8,128)(2,1)}, f32[8,128]{1,0:T(8,128)}) custom-call(bf16[128,4096]{1,0:T(8,128)(2,1)} %q_hbm.1, bf16[128,512]{1,0:T(8,128)(2,1)} %k_hbm.1, bf16[128,512]{1,0:T(8,128)(2,1)} %v_hbm.1, bf16[128,4096]{1,0:T(8,128)(2,1)} %do_hbm.1, ...), custom_call_target="tpu_custom_call" | custom-call | tf_op jit(solution)/shard_map/tree_attention/pallas_call | solution.py:505
  53.0 3.0 %finish.1 = (bf16[128,4096]{1,0:T(8,128)(2,1)}, bf16[128,4096]{1,0:T(8,128)(2,1)}, bf16[128,512]{1,0:T(8,128)(2,1)}, bf16[128,512]{1,0:T(8,128)(2,1)}, f32[1]{0:T(128)}) custom-call(bf16[128,4096]{1,0:T(8,128)(2,1)} %get-tuple-element.10.refs_0_, bf16[128,4096]{1,0:T(8,128)(2,1)} %get-tuple-element.11.refs_1_, bf16[128,512]{1,0:T(8,128)(2,1)} %get-tuple-element.12.refs_2_, ...), custom_call_target="tpu_custom_call" | custom-call | tf_op jit(solution)/shard_map/finish/pallas_call | solution.py:547
